TPU v7x, 32 devices: a whole 2x2x4 slice. The times are simulated.
32 devices in a mesh: req: 16 (over z, x, core), tp: 2 (over y).
Axes of the slice: x: 2, y: 2, z: 4, core: 2. Of those that a mesh axis runs over, the one named last changes fastest.
Arguments:
- queries: bfloat16 [6144, 8192], P('req', 'tp'), may hold values from -40 to 40
- suffix_kv: bfloat16 [2, 6144, 1024], P(None, 'req', 'tp'), may hold values from -4 to 4
- prefix_kv: bfloat16 [2, 16, 256, 1024], P(None, 'req', 'tp'), may hold values from -4 to 4
- suffix_length: int32 [15], replicated, may hold values from 16 to 384, as said below
- request_group: int32 [15], replicated, may hold values from 0 to 3
- request_order: int32 [15], replicated, may hold values from 0 to 14, each once
- owner_map: int32 [16], replicated, may hold values from 0 to 15, each once
Outputs:
- attention: bfloat16 [6144, 8192], P('req', 'tp')
Inputs may be any that keep to these rules, and one draw needn't show every extreme that they name: `suffix_length`: every suffix has 16 to 384 tokens; in every draw one suffix has exactly 384 tokens and one exactly 16.
All inputs are finite; a program needn't handle non-finite values.
Results may differ from a plain program's by a relative error of at most 0.007.
Values may be sent and summed in bfloat16 or wider, within the bound.
A program may use at most 128 MiB of HBM per device.

v0:
```python
import math

import jax
import jax.numpy as jnp
from jax import lax
from jax.sharding import PartitionSpec as P

QH = 64
KVH = 8
HD = 128
GROUPS = 4


masked_score = -1e30


def from_behind(block, axis, distance):
    devices = range(lax.axis_size(axis))
    route = [(i - distance, i) for i in devices if i - distance in devices]
    return lax.ppermute(block, axis, route)


def pack_index(slot_ids, starts, stops):
    inside = (starts[None, :] <= slot_ids[:, None]) & (slot_ids[:, None] < stops[None, :])
    request_ids = jnp.arange(starts.shape[0], dtype=jnp.int32)
    found = jnp.sum(jnp.where(inside, request_ids[None, :], 0), axis=1)
    missing = jnp.where(jnp.any(inside, axis=1), 0, starts.shape[0]).astype(jnp.int32)
    return found + missing


def pick_rows(lookup, selector, extent):
    matches = selector[:, None] == jnp.arange(extent, dtype=jnp.int32)[None, :]
    return jnp.sum(jnp.where(matches, lookup[None, :], 0), axis=1)


def per_device(
    queries, suffix_kv, prefix_kv, suffix_length, request_group, request_order, owner_map
):
    tok_rows = queries.shape[0]
    head_cols = suffix_kv.shape[2]
    kv_heads = head_cols // HD
    per_kv = QH // KVH
    stored_count = owner_map.shape[0]
    per_group = stored_count // GROUPS
    requests = suffix_length.shape[0]
    score_scale = 1.0 / math.sqrt(HD)
    packed_length = pick_rows(suffix_length, request_order, requests)
    packed_group = pick_rows(request_group, request_order, requests)
    starts = (jnp.arange(requests, dtype=jnp.int32) + 1) * tok_rows - packed_length // 2
    stops = starts + packed_length
    device = lax.axis_index("req")
    slot_ids = device * tok_rows + jnp.arange(tok_rows, dtype=jnp.int32)
    own_pack = pack_index(slot_ids, starts, stops)
    is_live = own_pack < requests
    slot_group = pick_rows(packed_group, own_pack, requests)
    block_ids = jnp.arange(stored_count, dtype=jnp.int32)
    stored_group = jnp.sum(
        jnp.where(owner_map[None, :] == block_ids[:, None], (block_ids // per_group)[None, :], 0),
        axis=1,
    )
    query_heads = queries.reshape(tok_rows, kv_heads, per_kv, HD)

    def absorb(carried, key_rows, value_rows, allowed):
        running_max, running_sum, running_acc = carried
        scores = (
            jnp.einsum("tjqd,kjd->jtqk", query_heads, key_rows, preferred_element_type=jnp.float32)
            * score_scale
        )
        visible = allowed[None, :, None, :]
        scores = jnp.where(visible, scores, masked_score)
        new_max = jnp.maximum(running_max, jnp.max(scores, axis=-1))
        weights = jnp.where(visible, jnp.exp(scores - new_max[..., None]), 0.0)
        shrink = jnp.exp(running_max - new_max)
        new_sum = running_sum * shrink + jnp.sum(weights, axis=-1)
        product = jnp.einsum(
            "jtqk,kjd->jtqd",
            weights.astype(jnp.bfloat16),
            value_rows,
            preferred_element_type=jnp.float32,
        )
        return (new_max, new_sum, running_acc * shrink[..., None] + product)

    earlier = from_behind(suffix_kv, "req", 1)
    nearby = jnp.concatenate([earlier, suffix_kv], axis=1)
    near_slots = device * tok_rows - tok_rows + jnp.arange(2 * tok_rows, dtype=jnp.int32)
    near_pack = pack_index(near_slots, starts, stops)
    near_allowed = (
        (near_pack[None, :] == own_pack[:, None])
        & (near_slots[None, :] <= slot_ids[:, None])
        & (near_slots[None, :] >= 0)
        & is_live[:, None]
    )
    initial = (
        jnp.full((kv_heads, tok_rows, per_kv), masked_score, jnp.float32),
        jnp.zeros((kv_heads, tok_rows, per_kv), jnp.float32),
        jnp.zeros((kv_heads, tok_rows, per_kv, HD), jnp.float32),
    )
    carried = absorb(
        initial,
        nearby[0].reshape(2 * tok_rows, kv_heads, HD),
        nearby[1].reshape(2 * tok_rows, kv_heads, HD),
        near_allowed,
    )
    stored = lax.all_gather(prefix_kv, "req", axis=1, tiled=True)
    relaid = lax.all_to_all(stored, "tp", split_axis=3, concat_axis=2, tiled=True)
    status = carried
    extent = relaid.shape[1]
    block_rows = relaid.shape[2]
    stride = math.gcd(extent, max(1, 512 // block_rows))
    passes = extent // stride
    key_rows = relaid[0].reshape(passes, stride * block_rows, kv_heads, HD)
    value_rows = relaid[1].reshape(passes, stride * block_rows, kv_heads, HD)
    key_groups = jnp.repeat(stored_group, block_rows).reshape(passes, stride * block_rows)

    def visit_block(inner, inputs):
        keys_here, values_here, groups_here = inputs
        allowed = (groups_here[None, :] == slot_group[:, None]) & is_live[:, None]
        inner = absorb(inner, keys_here, values_here, allowed)
        return (inner, None)

    status, unused = lax.scan(visit_block, status, (key_rows, value_rows, key_groups))
    carried = status
    running_max, running_sum, running_acc = carried
    divisor = jnp.where(is_live[None, :, None], running_sum, 1.0)
    result = jnp.where(is_live[None, :, None, None], running_acc / divisor[..., None], 0.0)
    return (
        jnp.transpose(result, (1, 0, 2, 3))
        .reshape(tok_rows, kv_heads * per_kv * HD)
        .astype(jnp.bfloat16)
    )


def solution(mesh):
    in_specs = (
        P("req", "tp"),
        P(None, "req", "tp"),
        P(None, "req", "tp", None),
        P(),
        P(),
        P(),
        P(),
    )
    out_specs = P("req", "tp")
    return jax.shard_map(
        per_device, mesh=mesh, in_specs=in_specs, out_specs=out_specs, check_vma=False
    )
```

profile of v0, /device:TPU:1, one launch (start us, length us, event | category | flops | bytes accessed | tf_op | source)
XLA Modules:
  0.0 588.3 jit_solution(2074436803383109382)
XLA Ops:
  6.6 0.7 all-gather.2.cloned.1.call-update
  7.3 2.3 copy.58
  9.6 4.5 collective-permute-start
  14.1 4.6 copy.60
  18.7 3.6 copy.70
  23.4 0.8 and_and_fusion
  24.2 4.3 collective-permute-done
  28.5 2.4 pad_maximum_fusion
  30.9 17.3 %fusion.12 = (f32[4,384,8]{1,2,0:T(8,128)S(1)}, f32[4,768,384,8]{2,1,3,0:T(8,128)}) fusion(pred[384,768]{0,1:T(8,128)(4,1)S(1)} %and_and_fusion, bf16[768,4,128,1]{0,2,3,1:T(8,128)(2,1)S(1)} %bitcast.89, bf16[384,4,8,128]{0,3,2,1:T(8,128)(2,1)} %bitcast.87), kind=kOutput, calls=%fused_computation.22 | convolution fusion | flops 2444218368 | bytes 42024960 | tf_op jit(solution)/shard_map/tjqd,kjd->jtqk/dot_general | solution.py:66
  48.8 40.6 %all-gather.2.cloned.1.call-done = bf16[2,16,128,1024]{3,2,0,1:T(8,128)(2,1)} async-done(((bf16[2,1,128,1024]{3,2,0,1:T(8,128)(2,1)}), bf16[2,16,128,1024]{3,2,0,1:T(8,128)(2,1)}) %all-gather.2.cloned.1.call-update) | async-done | bytes 8388624 | tf_op jit(solution)/shard_map/all_gather | solution.py:104
  89.4 12.6 %copy.67 = bf16[2,16,128,1024]{2,1,0,3:T(8,128)(2,1)} copy(bf16[2,16,128,1024]{3,2,0,1:T(8,128)(2,1)} %all-gather.2.cloned.1.call-done) | data formatting | bytes 16777216 | tf_op jit(solution)/shard_map/all_gather | solution.py:104
  102.0 7.1 %all-to-all-start = ((bf16[2,16,128,1024]{2,1,0,3:T(8,128)(2,1)}), bf16[2,16,128,1024]{2,1,0,3:T(8,128)(2,1)}, u32[]{:S(2)}, u32[]{:S(2)}) async-start(bf16[2,16,128,1024]{2,1,0,3:T(8,128)(2,1)} %copy.67), calls=%async_computation | async-start | bytes 16777216 | tf_op jit(solution)/shard_map/all_to_all | solution.py:105
  109.1 16.9 %fusion.14 = f32[4,384,8]{1,2,0:T(8,128)S(1)} fusion(f32[4,768,384,8]{2,1,3,0:T(8,128)} %get-tuple-element.139, f32[4,384,8]{1,2,0:T(8,128)S(1)} %broadcast_maximum_fusion, pred[384,768]{0,1:T(8,128)(4,1)S(1)} %and_and_fusion), kind=kLoop, calls=%fused_computation.24 | loop fusion | flops 47173632 | bytes 38141952 | tf_op jit(solution)/shard_map/reduce_sum | solution.py:74
  126.1 20.1 %broadcast_add_fusion = f32[4,384,8,128]{3,1,2,0:T(8,128)} fusion(f32[4,384,8]{1,2,0:T(8,128)S(1)} %get-tuple-element.136, bf16[768,4,128,1]{0,2,3,1:T(8,128)(2,1)S(1)} %bitcast.90, f32[4,768,384,8]{2,1,3,0:T(8,128)} %get-tuple-element.139, f32[4,384,8]{1,2,0:T(8,128)S(1)} %broadcast_maximum_fusion, pred[384,768]{0,1:T(8,128)(4,1)S(1)} %and_and_fusion), kind=kOutput, calls=%fused_computation.29 | convolution fusion | flops 2464677888 | bytes 45219840 | tf_op jit(solution)/shard_map/jtqk,kjd->jtqd/dot_general | solution.py:75
  146.2 55.0 %all-to-all-done = bf16[2,16,128,1024]{2,1,0,3:T(8,128)(2,1)} async-done(((bf16[2,16,128,1024]{2,1,0,3:T(8,128)(2,1)}), bf16[2,16,128,1024]{2,1,0,3:T(8,128)(2,1)}, u32[]{:S(2)}, u32[]{:S(2)}) %all-to-all-start) | async-done | bytes 8388640 | tf_op jit(solution)/shard_map/all_to_all | solution.py:105
  201.2 13.8 %copy.68 = bf16[2,16,128,2,512]{4,2,3,1,0:T(8,128)(2,1)} copy(bf16[2,16,128,2,512]{2,1,0,4,3:T(8,128)(2,1)} %bitcast.16) | data formatting | bytes 16777216 | tf_op jit(solution)/shard_map/all_to_all | solution.py:105
  215.0 5.9 fusion.31
  220.9 6.9 %reshape_squeeze.14 = bf16[8,512,4,128]{3,2,1,0:T(4,128)(2,1)} reshape(bf16[1,16,2,128,512]{4,3,2,1,0:T(8,128)(2,1)} %get-tuple-element.133) | data formatting | bytes 8388608 | tf_op jit(solution)/shard_map/reshape;squeeze | solution.py:111
  227.8 6.9 %reshape_squeeze.15 = bf16[8,512,4,128]{3,2,1,0:T(4,128)(2,1)} reshape(bf16[1,16,2,128,512]{4,3,2,1,0:T(8,128)(2,1)} %get-tuple-element.132) | data formatting | bytes 8388608 | tf_op jit(solution)/shard_map/reshape;squeeze | solution.py:112
  234.7 0.7 broadcast_in_dim.211
  235.4 336.0 %while.14 = (s32[]{:T(128)}, f32[4,384,8]{1,2,0:T(8,128)S(1)}, f32[4,384,8]{1,2,0:T(8,128)S(1)}, f32[4,384,8,128]{3,1,2,0:T(8,128)}, s32[8,512]{1,0:T(8,128)}, /...) while((s32[]{:T(128)}, f32[4,384,8]{1,2,0:T(8,128)S(1)}, ...), condition=%wide.region_13.14_spmd, body=%wide.region_10.13_spmd.sunk | while | flops 3306577920 | bytes 95952880 | solution.py:121
  235.4 0.7 constant_dynamic-slice_fusion.5
  236.3 2.4 constant_dynamic-slice_fusion.6
  238.7 10.3 %fusion.42 = (f32[4,384,8]{1,2,0:T(8,128)S(1)}, f32[4,512,384,8]{2,1,3,0:T(8,128)}) fusion(pred[384,512]{0,1:T(8,128)(4,1)S(1)} %compare_and_fusion.4, bf16[384,4,8,128]{3,0,2,1:T(8,128)(2,1)S(1)} %get-tuple-element.243, bf16[1,512,4,128]{3,2,1,0:T(4,128)(2,1)S(1)} %get-tuple-element.207), kind=kOutput, calls=%fused_computation.2.clone.1 | convolution fusion | flops 1629474816 | bytes 29081600 | tf_op jit(solution)/shard_map/while/body/eval_jaxpr/tjqd,kjd->jtqk/dot_general | solution.py:66
  249.0 11.6 %fusion.43 = f32[4,384,8]{1,2,0:T(8,128)S(1)} fusion(f32[4,512,384,8]{2,1,3,0:T(8,128)} %get-tuple-element.209, f32[4,384,8]{1,2,0:T(8,128)S(1)} %max.4, pred[384,512]{0,1:T(8,128)(4,1)S(1)} %compare_and_fusion.4), kind=kLoop, calls=%fused_computation.4.clone.1 | loop fusion | flops 31444992 | bytes 25460736 | tf_op jit(solution)/shard_map/while/body/eval_jaxpr/reduce_sum | solution.py:74
  261.2 16.2 %multiply_add_fusion.5 = f32[4,384,8,128]{3,1,2,0:T(8,128)} fusion(f32[4,384,8,128]{3,1,2,0:T(8,128)} %get-tuple-element.227, f32[4,384,8]{1,2,0:T(8,128)} %get-tuple-element.211, f32[4,512,384,8]{2,1,3,0:T(8,128)} %get-tuple-element.209, f32[4,384,8]{1,2,0:T(8,128)S(1)} %max.4, pred[384,512]{0,1:T(8,128)(4,1)S(1)} %compare_and_fusion.4, ...), kind=kOutput, calls=%fused_computation.7.clone.1 | convolution fusion | flops 1645215744 | bytes 38567936 | tf_op jit(solution)/shard_map/while/body/eval_jaxpr/jtqk,kjd->jtqd/dot_general | solution.py:75
  277.4 0.7 constant_dynamic-slice_fusion.5
  278.3 2.4 constant_dynamic-slice_fusion.6
  280.7 10.3 %fusion.42 = (f32[4,384,8]{1,2,0:T(8,128)S(1)}, f32[4,512,384,8]{2,1,3,0:T(8,128)}) fusion(pred[384,512]{0,1:T(8,128)(4,1)S(1)} %compare_and_fusion.4, bf16[384,4,8,128]{3,0,2,1:T(8,128)(2,1)S(1)} %get-tuple-element.243, bf16[1,512,4,128]{3,2,1,0:T(4,128)(2,1)S(1)} %get-tuple-element.207), kind=kOutput, calls=%fused_computation.2.clone.1 | convolution fusion | flops 1629474816 | bytes 29081600 | tf_op jit(solution)/shard_map/while/body/eval_jaxpr/tjqd,kjd->jtqk/dot_general | solution.py:66
  291.0 11.6 %fusion.43 = f32[4,384,8]{1,2,0:T(8,128)S(1)} fusion(f32[4,512,384,8]{2,1,3,0:T(8,128)} %get-tuple-element.209, f32[4,384,8]{1,2,0:T(8,128)S(1)} %max.4, pred[384,512]{0,1:T(8,128)(4,1)S(1)} %compare_and_fusion.4), kind=kLoop, calls=%fused_computation.4.clone.1 | loop fusion | flops 31444992 | bytes 25460736 | tf_op jit(solution)/shard_map/while/body/eval_jaxpr/reduce_sum | solution.py:74
  303.2 16.2 %multiply_add_fusion.5 = f32[4,384,8,128]{3,1,2,0:T(8,128)} fusion(f32[4,384,8,128]{3,1,2,0:T(8,128)} %get-tuple-element.227, f32[4,384,8]{1,2,0:T(8,128)} %get-tuple-element.211, f32[4,512,384,8]{2,1,3,0:T(8,128)} %get-tuple-element.209, f32[4,384,8]{1,2,0:T(8,128)S(1)} %max.4, pred[384,512]{0,1:T(8,128)(4,1)S(1)} %compare_and_fusion.4, ...), kind=kOutput, calls=%fused_computation.7.clone.1 | convolution fusion | flops 1645215744 | bytes 38567936 | tf_op jit(solution)/shard_map/while/body/eval_jaxpr/jtqk,kjd->jtqd/dot_general | solution.py:75
  319.4 0.7 constant_dynamic-slice_fusion.5
  320.3 2.4 constant_dynamic-slice_fusion.6
  322.7 10.3 %fusion.42 = (f32[4,384,8]{1,2,0:T(8,128)S(1)}, f32[4,512,384,8]{2,1,3,0:T(8,128)}) fusion(pred[384,512]{0,1:T(8,128)(4,1)S(1)} %compare_and_fusion.4, bf16[384,4,8,128]{3,0,2,1:T(8,128)(2,1)S(1)} %get-tuple-element.243, bf16[1,512,4,128]{3,2,1,0:T(4,128)(2,1)S(1)} %get-tuple-element.207), kind=kOutput, calls=%fused_computation.2.clone.1 | convolution fusion | flops 1629474816 | bytes 29081600 | tf_op jit(solution)/shard_map/while/body/eval_jaxpr/tjqd,kjd->jtqk/dot_general | solution.py:66
  333.0 11.6 %fusion.43 = f32[4,384,8]{1,2,0:T(8,128)S(1)} fusion(f32[4,512,384,8]{2,1,3,0:T(8,128)} %get-tuple-element.209, f32[4,384,8]{1,2,0:T(8,128)S(1)} %max.4, pred[384,512]{0,1:T(8,128)(4,1)S(1)} %compare_and_fusion.4), kind=kLoop, calls=%fused_computation.4.clone.1 | loop fusion | flops 31444992 | bytes 25460736 | tf_op jit(solution)/shard_map/while/body/eval_jaxpr/reduce_sum | solution.py:74
  345.2 16.2 %multiply_add_fusion.5 = f32[4,384,8,128]{3,1,2,0:T(8,128)} fusion(f32[4,384,8,128]{3,1,2,0:T(8,128)} %get-tuple-element.227, f32[4,384,8]{1,2,0:T(8,128)} %get-tuple-element.211, f32[4,512,384,8]{2,1,3,0:T(8,128)} %get-tuple-element.209, f32[4,384,8]{1,2,0:T(8,128)S(1)} %max.4, pred[384,512]{0,1:T(8,128)(4,1)S(1)} %compare_and_fusion.4, ...), kind=kOutput, calls=%fused_computation.7.clone.1 | convolution fusion | flops 1645215744 | bytes 38567936 | tf_op jit(solution)/shard_map/while/body/eval_jaxpr/jtqk,kjd->jtqd/dot_general | solution.py:75
  361.4 0.7 constant_dynamic-slice_fusion.5
  362.3 2.4 constant_dynamic-slice_fusion.6
  364.7 10.3 %fusion.42 = (f32[4,384,8]{1,2,0:T(8,128)S(1)}, f32[4,512,384,8]{2,1,3,0:T(8,128)}) fusion(pred[384,512]{0,1:T(8,128)(4,1)S(1)} %compare_and_fusion.4, bf16[384,4,8,128]{3,0,2,1:T(8,128)(2,1)S(1)} %get-tuple-element.243, bf16[1,512,4,128]{3,2,1,0:T(4,128)(2,1)S(1)} %get-tuple-element.207), kind=kOutput, calls=%fused_computation.2.clone.1 | convolution fusion | flops 1629474816 | bytes 29081600 | tf_op jit(solution)/shard_map/while/body/eval_jaxpr/tjqd,kjd->jtqk/dot_general | solution.py:66
  375.0 11.6 %fusion.43 = f32[4,384,8]{1,2,0:T(8,128)S(1)} fusion(f32[4,512,384,8]{2,1,3,0:T(8,128)} %get-tuple-element.209, f32[4,384,8]{1,2,0:T(8,128)S(1)} %max.4, pred[384,512]{0,1:T(8,128)(4,1)S(1)} %compare_and_fusion.4), kind=kLoop, calls=%fused_computation.4.clone.1 | loop fusion | flops 31444992 | bytes 25460736 | tf_op jit(solution)/shard_map/while/body/eval_jaxpr/reduce_sum | solution.py:74
  387.2 16.2 %multiply_add_fusion.5 = f32[4,384,8,128]{3,1,2,0:T(8,128)} fusion(f32[4,384,8,128]{3,1,2,0:T(8,128)} %get-tuple-element.227, f32[4,384,8]{1,2,0:T(8,128)} %get-tuple-element.211, f32[4,512,384,8]{2,1,3,0:T(8,128)} %get-tuple-element.209, f32[4,384,8]{1,2,0:T(8,128)S(1)} %max.4, pred[384,512]{0,1:T(8,128)(4,1)S(1)} %compare_and_fusion.4, ...), kind=kOutput, calls=%fused_computation.7.clone.1 | convolution fusion | flops 1645215744 | bytes 38567936 | tf_op jit(solution)/shard_map/while/body/eval_jaxpr/jtqk,kjd->jtqd/dot_general | solution.py:75
  403.4 0.7 constant_dynamic-slice_fusion.5
  404.3 2.4 constant_dynamic-slice_fusion.6
  406.7 10.3 %fusion.42 = (f32[4,384,8]{1,2,0:T(8,128)S(1)}, f32[4,512,384,8]{2,1,3,0:T(8,128)}) fusion(pred[384,512]{0,1:T(8,128)(4,1)S(1)} %compare_and_fusion.4, bf16[384,4,8,128]{3,0,2,1:T(8,128)(2,1)S(1)} %get-tuple-element.243, bf16[1,512,4,128]{3,2,1,0:T(4,128)(2,1)S(1)} %get-tuple-element.207), kind=kOutput, calls=%fused_computation.2.clone.1 | convolution fusion | flops 1629474816 | bytes 29081600 | tf_op jit(solution)/shard_map/while/body/eval_jaxpr/tjqd,kjd->jtqk/dot_general | solution.py:66
  417.0 11.6 %fusion.43 = f32[4,384,8]{1,2,0:T(8,128)S(1)} fusion(f32[4,512,384,8]{2,1,3,0:T(8,128)} %get-tuple-element.209, f32[4,384,8]{1,2,0:T(8,128)S(1)} %max.4, pred[384,512]{0,1:T(8,128)(4,1)S(1)} %compare_and_fusion.4), kind=kLoop, calls=%fused_computation.4.clone.1 | loop fusion | flops 31444992 | bytes 25460736 | tf_op jit(solution)/shard_map/while/body/eval_jaxpr/reduce_sum | solution.py:74
  429.2 16.2 %multiply_add_fusion.5 = f32[4,384,8,128]{3,1,2,0:T(8,128)} fusion(f32[4,384,8,128]{3,1,2,0:T(8,128)} %get-tuple-element.227, f32[4,384,8]{1,2,0:T(8,128)} %get-tuple-element.211, f32[4,512,384,8]{2,1,3,0:T(8,128)} %get-tuple-element.209, f32[4,384,8]{1,2,0:T(8,128)S(1)} %max.4, pred[384,512]{0,1:T(8,128)(4,1)S(1)} %compare_and_fusion.4, ...), kind=kOutput, calls=%fused_computation.7.clone.1 | convolution fusion | flops 1645215744 | bytes 38567936 | tf_op jit(solution)/shard_map/while/body/eval_jaxpr/jtqk,kjd->jtqd/dot_general | solution.py:75
  445.4 0.7 constant_dynamic-slice_fusion.5
  446.3 2.4 constant_dynamic-slice_fusion.6
  448.7 10.3 %fusion.42 = (f32[4,384,8]{1,2,0:T(8,128)S(1)}, f32[4,512,384,8]{2,1,3,0:T(8,128)}) fusion(pred[384,512]{0,1:T(8,128)(4,1)S(1)} %compare_and_fusion.4, bf16[384,4,8,128]{3,0,2,1:T(8,128)(2,1)S(1)} %get-tuple-element.243, bf16[1,512,4,128]{3,2,1,0:T(4,128)(2,1)S(1)} %get-tuple-element.207), kind=kOutput, calls=%fused_computation.2.clone.1 | convolution fusion | flops 1629474816 | bytes 29081600 | tf_op jit(solution)/shard_map/while/body/eval_jaxpr/tjqd,kjd->jtqk/dot_general | solution.py:66
  459.0 11.6 %fusion.43 = f32[4,384,8]{1,2,0:T(8,128)S(1)} fusion(f32[4,512,384,8]{2,1,3,0:T(8,128)} %get-tuple-element.209, f32[4,384,8]{1,2,0:T(8,128)S(1)} %max.4, pred[384,512]{0,1:T(8,128)(4,1)S(1)} %compare_and_fusion.4), kind=kLoop, calls=%fused_computation.4.clone.1 | loop fusion | flops 31444992 | bytes 25460736 | tf_op jit(solution)/shard_map/while/body/eval_jaxpr/reduce_sum | solution.py:74
  471.2 16.2 %multiply_add_fusion.5 = f32[4,384,8,128]{3,1,2,0:T(8,128)} fusion(f32[4,384,8,128]{3,1,2,0:T(8,128)} %get-tuple-element.227, f32[4,384,8]{1,2,0:T(8,128)} %get-tuple-element.211, f32[4,512,384,8]{2,1,3,0:T(8,128)} %get-tuple-element.209, f32[4,384,8]{1,2,0:T(8,128)S(1)} %max.4, pred[384,512]{0,1:T(8,128)(4,1)S(1)} %compare_and_fusion.4, ...), kind=kOutput, calls=%fused_computation.7.clone.1 | convolution fusion | flops 1645215744 | bytes 38567936 | tf_op jit(solution)/shard_map/while/body/eval_jaxpr/jtqk,kjd->jtqd/dot_general | solution.py:75
  487.4 0.7 constant_dynamic-slice_fusion.5
  488.3 2.4 constant_dynamic-slice_fusion.6
  490.7 10.3 %fusion.42 = (f32[4,384,8]{1,2,0:T(8,128)S(1)}, f32[4,512,384,8]{2,1,3,0:T(8,128)}) fusion(pred[384,512]{0,1:T(8,128)(4,1)S(1)} %compare_and_fusion.4, bf16[384,4,8,128]{3,0,2,1:T(8,128)(2,1)S(1)} %get-tuple-element.243, bf16[1,512,4,128]{3,2,1,0:T(4,128)(2,1)S(1)} %get-tuple-element.207), kind=kOutput, calls=%fused_computation.2.clone.1 | convolution fusion | flops 1629474816 | bytes 29081600 | tf_op jit(solution)/shard_map/while/body/eval_jaxpr/tjqd,kjd->jtqk/dot_general | solution.py:66
  501.0 11.6 %fusion.43 = f32[4,384,8]{1,2,0:T(8,128)S(1)} fusion(f32[4,512,384,8]{2,1,3,0:T(8,128)} %get-tuple-element.209, f32[4,384,8]{1,2,0:T(8,128)S(1)} %max.4, pred[384,512]{0,1:T(8,128)(4,1)S(1)} %compare_and_fusion.4), kind=kLoop, calls=%fused_computation.4.clone.1 | loop fusion | flops 31444992 | bytes 25460736 | tf_op jit(solution)/shard_map/while/body/eval_jaxpr/reduce_sum | solution.py:74
  513.2 16.2 %multiply_add_fusion.5 = f32[4,384,8,128]{3,1,2,0:T(8,128)} fusion(f32[4,384,8,128]{3,1,2,0:T(8,128)} %get-tuple-element.227, f32[4,384,8]{1,2,0:T(8,128)} %get-tuple-element.211, f32[4,512,384,8]{2,1,3,0:T(8,128)} %get-tuple-element.209, f32[4,384,8]{1,2,0:T(8,128)S(1)} %max.4, pred[384,512]{0,1:T(8,128)(4,1)S(1)} %compare_and_fusion.4, ...), kind=kOutput, calls=%fused_computation.7.clone.1 | convolution fusion | flops 1645215744 | bytes 38567936 | tf_op jit(solution)/shard_map/while/body/eval_jaxpr/jtqk,kjd->jtqd/dot_general | solution.py:75
  529.4 0.7 constant_dynamic-slice_fusion.5
  530.3 2.4 constant_dynamic-slice_fusion.6
  532.7 10.3 %fusion.42 = (f32[4,384,8]{1,2,0:T(8,128)S(1)}, f32[4,512,384,8]{2,1,3,0:T(8,128)}) fusion(pred[384,512]{0,1:T(8,128)(4,1)S(1)} %compare_and_fusion.4, bf16[384,4,8,128]{3,0,2,1:T(8,128)(2,1)S(1)} %get-tuple-element.243, bf16[1,512,4,128]{3,2,1,0:T(4,128)(2,1)S(1)} %get-tuple-element.207), kind=kOutput, calls=%fused_computation.2.clone.1 | convolution fusion | flops 1629474816 | bytes 29081600 | tf_op jit(solution)/shard_map/while/body/eval_jaxpr/tjqd,kjd->jtqk/dot_general | solution.py:66
  543.0 11.6 %fusion.43 = f32[4,384,8]{1,2,0:T(8,128)S(1)} fusion(f32[4,512,384,8]{2,1,3,0:T(8,128)} %get-tuple-element.209, f32[4,384,8]{1,2,0:T(8,128)S(1)} %max.4, pred[384,512]{0,1:T(8,128)(4,1)S(1)} %compare_and_fusion.4), kind=kLoop, calls=%fused_computation.4.clone.1 | loop fusion | flops 31444992 | bytes 25460736 | tf_op jit(solution)/shard_map/while/body/eval_jaxpr/reduce_sum | solution.py:74
  555.2 16.2 %multiply_add_fusion.5 = f32[4,384,8,128]{3,1,2,0:T(8,128)} fusion(f32[4,384,8,128]{3,1,2,0:T(8,128)} %get-tuple-element.227, f32[4,384,8]{1,2,0:T(8,128)} %get-tuple-element.211, f32[4,512,384,8]{2,1,3,0:T(8,128)} %get-tuple-element.209, f32[4,384,8]{1,2,0:T(8,128)S(1)} %max.4, pred[384,512]{0,1:T(8,128)(4,1)S(1)} %compare_and_fusion.4, ...), kind=kOutput, calls=%fused_computation.7.clone.1 | convolution fusion | flops 1645215744 | bytes 38567936 | tf_op jit(solution)/shard_map/while/body/eval_jaxpr/jtqk,kjd->jtqd/dot_general | solution.py:75
  571.4 4.8 fusion.18
  576.2 2.0 copy.72
  578.3 3.2 copy.94
  (66 shorter events, 8.3 us)
Async XLA Ops:
  6.5 15.8 %copy-start.6 = (s32[16]{0:T(128)S(1)}, s32[16]{0:T(128)}, u32[]{:S(2)}) copy-start(s32[16]{0:T(128)} %param.15) | copy-start | bytes 196
  6.5 16.1 %copy-start.5 = (s32[15]{0:T(128)S(1)}, s32[15]{0:T(128)}, u32[]{:S(2)}) copy-start(s32[15]{0:T(128)} %param.12) | copy-start | bytes 184
  6.5 16.1 %copy-start.3 = (s32[15]{0:T(128)S(1)}, s32[15]{0:T(128)}, u32[]{:S(2)}) copy-start(s32[15]{0:T(128)} %param.13) | copy-start | bytes 184
  6.5 16.2 %copy-start.4 = (s32[15]{0:T(128)S(1)}, s32[15]{0:T(128)}, u32[]{:S(2)}) copy-start(s32[15]{0:T(128)} %param.14) | copy-start | bytes 184
  6.5 82.9 %all-gather.2.cloned.1.call-start = ((), (), s32[]{:S(2)}) async-start(), calls=%async_computation.1 | async-start | bytes 8912896 | tf_op jit(solution)/shard_map/all_gather | solution.py:104
  9.6 18.9 %collective-permute-start = (bf16[2,384,512]{1,2,0:T(8,128)(2,1)}, bf16[2,384,512]{1,2,0:T(8,128)(2,1)}, u32[]{:S(2)}, u32[]{:S(2)}) collective-permute-start(bf16[2,384,512]{1,2,0:T(8,128)(2,1)} %copy.58), channel_id=1, source_target_pairs={{0,2},{2,4},{4,6},{6,8},{8,10},{10,12},{12,14},{14,16},{16,18},{18... | collective-permute-start | bytes 2359304 | tf_op jit(solution)/shard_map/ppermute | solution.py:20
  48.1 0.6 copy-start.1
  102.0 99.2 %all-to-all-start = ((bf16[2,16,128,1024]{2,1,0,3:T(8,128)(2,1)}), bf16[2,16,128,1024]{2,1,0,3:T(8,128)(2,1)}, u32[]{:S(2)}, u32[]{:S(2)}) async-start(bf16[2,16,128,1024]{2,1,0,3:T(8,128)(2,1)} %copy.67), calls=%async_computation | async-start | bytes 16777216 | tf_op jit(solution)/shard_map/all_to_all | solution.py:105
  109.1 16.9 %copy-start.2 = (f32[4,384,8]{1,2,0:T(8,128)S(1)}, f32[4,384,8]{1,2,0:T(8,128)}, u32[]{:S(2)}) copy-start(f32[4,384,8]{1,2,0:T(8,128)} %copy-done.1) | copy-start | bytes 147460
  109.1 16.9 %copy-start = (bf16[1,768,512]{1,2,0:T(8,128)(2,1)S(1)}, bf16[1,768,512]{1,2,0:T(8,128)(2,1)}, u32[]{:S(2)}) copy-start(bf16[1,768,512]{1,2,0:T(8,128)(2,1)} %get-tuple-element.134) | copy-start | bytes 2359300
Sparse Core Ops, SparseCore 0:
  9.5 79.8 all-gather.1
where the time goes:
time: 592 us; the launch traced here: 588 us
  matrix products  249 us (42%)
  other arithmetic  125 us (21%)
  waiting for transfers between devices  101 us (17%)
  local copies, waits for them, and re-layouts  88.1 us (15%)
  between operations  13.6 us (2%)
  starting transfers between devices  11.7 us (2%)
    dot_general x9, matrix products, absorb(): jnp.einsum('jtqk,kjd->jtqd', weights.astype(jnp.bfloat16), value_rows, pr...  149 us
    reduce_sum x9, other arithmetic, absorb(): new_sum = running_sum * shrink + jnp.sum(weights, axis=-1)  110 us
    dot_general x9, matrix products, absorb(): jnp.einsum('tjqd,kjd->jtqk', query_heads, key_rows, preferred_element_typ...  99.8 us
    all_to_all x1, waiting for transfers between devices, per_device(): lax.all_to_all(stored, 'tp', split_axis=3, concat_axis=2, tiled=True)  55 us
    all_gather x1, waiting for transfers between devices, per_device(): stored = lax.all_gather(prefix_kv, 'req', axis=1, tiled=True)  40.6 us
    dynamic_slice x16, local copies, waits for them, and re-layouts, per_device(): lax.scan(visit_block, status, (key_rows, value_rows, key_groups))  24.7 us
    all_to_all x1, local copies, waits for them, and re-layouts, per_device(): lax.all_to_all(stored, 'tp', split_axis=3, concat_axis=2, tiled=True)  13.8 us
    all_gather x1, local copies, waits for them, and re-layouts, per_device(): stored = lax.all_gather(prefix_kv, 'req', axis=1, tiled=True)  12.6 us
  transfers between devices with their start and end apart: 3, of which 3 were waited for; matrix products, arithmetic and copies ran while one was open for 12% of the time, Pallas kernels for 0%

commit v1 on v0

v1 whole, which is shorter than its diff:
```python
import functools
import math

import jax
import jax.numpy as jnp
from jax import lax
from jax.experimental import pallas as pl
from jax.experimental.pallas import tpu as pltpu
from jax.sharding import PartitionSpec as P

QH = 64
KVH = 8
HD = 128
GROUPS = 4
PER_KV = QH // KVH
PAIR = 2
UP, DOWN, ACROSS, SIBLING = range(4)

masked_score = -1e30
to_exp2 = math.log2(math.e) / math.sqrt(HD)


def nt_dot(a, b):
    return lax.dot_general(a, b, (((1,), (1,)), ((), ())), preferred_element_type=jnp.float32)


def kernel(
    reqs, tps, heads,
    queries, suffix, prefix, lengths, groups, order, owners,
    out,
    *scratch,
):
    stored = scratch[:heads]
    (before, key_stage, value_stage, bias,
     unit_send, unit_recv, peer_send, peer_recv, own_sem, before_send, before_recv) = scratch[heads:]
    me = lax.axis_index("req")
    tp = lax.axis_index("tp")
    layers = reqs // 4
    z, x, core = me // 4, (me // 2) % 2, me % 2
    half_rows = queries.shape[0] // 2
    block_rows = stored[0].shape[2]
    part_rows = block_rows // tps
    per_group = reqs // GROUPS
    prefix_rows = per_group * block_rows
    across = z * 4 + (1 - x) * 2 + core
    sibling = z * 4 + x * 2 + 1 - core
    targets = {UP: me + 4, DOWN: me - 4, ACROSS: across, SIBLING: sibling}

    barrier = pltpu.get_barrier_semaphore()

    def greet(there, **device):
        @pl.when(there)
        def _():
            pl.semaphore_signal(barrier, inc=1, device_id=device, device_id_type=pl.DeviceIdType.MESH)

        return jnp.where(there, 1, 0)

    met = (
        greet(z + 1 < layers, req=me + 4)
        + greet(z > 0, req=me - 4)
        + greet(z >= 0, req=across)
        + greet(z >= 0, req=sibling)
        + greet((core == 1) & (me + 1 < reqs), req=me + 1)
        + greet((core == 0) & (me > 0), req=me - 1)
    )
    for k in range(1, tps):
        met = met + greet(z >= 0, tp=(tp + k) % tps)
    pl.semaphore_wait(barrier, met)

    def unit_copy(h, block, way):
        return pltpu.make_async_remote_copy(
            src_ref=stored[h].at[block],
            dst_ref=stored[h].at[block],
            send_sem=unit_send.at[h, block, way],
            recv_sem=unit_recv.at[h, block],
            device_id={"req": targets[way]},
            device_id_type=pl.DeviceIdType.MESH,
        )

    def peer_copy(h, peer, part):
        columns = pl.ds(pl.multiple_of((peer * heads + h) * HD, HD), HD)
        return pltpu.make_async_remote_copy(
            src_ref=prefix.at[:, 0, :, columns],
            dst_ref=stored[h].at[me, :, pl.ds(pl.multiple_of(part * part_rows, part_rows), part_rows), :],
            send_sem=peer_send.at[h, peer],
            recv_sem=peer_recv.at[h, part],
            device_id={"tp": peer},
            device_id_type=pl.DeviceIdType.MESH,
        )

    def own_copy(h):
        columns = pl.ds(pl.multiple_of((tp * heads + h) * HD, HD), HD)
        return pltpu.make_async_copy(
            prefix.at[:, 0, :, columns],
            stored[h].at[me, :, pl.ds(pl.multiple_of(tp * part_rows, part_rows), part_rows), :],
            own_sem.at[h],
        )

    before_copy = pltpu.make_async_remote_copy(
        src_ref=suffix.at[:, pl.ds(half_rows, half_rows), :],
        dst_ref=before,
        send_sem=before_send,
        recv_sem=before_recv,
        device_id={"req": me + 1},
        device_id_type=pl.DeviceIdType.MESH,
    )

    def pass_on(h, block, ways):
        for way, there in ways:
            @pl.when(there)
            def _(way=way):
                unit_copy(h, block, way).start()

    def send_own(h):
        own_copy(h).wait()
        for k in range(1, tps):
            peer_copy(h, (tp + k) % tps, (tp + k) % tps).wait_recv()
        pass_on(h, me, [(UP, z + 1 < layers), (DOWN, z > 0), (ACROSS, z >= 0), (SIBLING, z >= 0)])

    def from_layer(h, step):
        below, above = z - step, z + step

        @pl.when(below >= 0)
        def _():
            block = me - 4 * step
            unit_copy(h, block, UP).wait_recv()
            pass_on(h, block, [(UP, z + 1 < layers), (ACROSS, z >= 0), (SIBLING, z >= 0)])

        @pl.when(above < layers)
        def _():
            block = me + 4 * step
            unit_copy(h, block, DOWN).wait_recv()
            pass_on(h, block, [(DOWN, z > 0), (ACROSS, z >= 0), (SIBLING, z >= 0)])

    def from_across(h, step):
        below, above = z - step, z + step

        @pl.when(below >= 0)
        def _():
            unit_copy(h, across - 4 * step, ACROSS).wait_recv()
            unit_copy(h, across - 4 * step, SIBLING).start()

        @pl.when((above < layers) & (step > 0))
        def _():
            unit_copy(h, across + 4 * step, ACROSS).wait_recv()
            unit_copy(h, across + 4 * step, SIBLING).start()

    def relay(h, step):
        @pl.when(step < layers)
        def _():
            from_layer(h, step)

        from_across(h, step - 1)

    def from_sibling(h):
        @pl.loop(0, reqs // 2)
        def _(i):
            unit_copy(h, i * 2 + 1 - core, SIBLING).wait_recv()

    for h in range(heads):
        own_copy(h).start()
        for k in range(1, tps):
            peer_copy(h, (tp + k) % tps, tp).start()
    send_own(0)

    @pl.when(me + 1 < reqs)
    def _():
        before_copy.start()

    if heads > 1:
        send_own(1)

    tail = order[jnp.maximum(me - 1, 0)]
    head = order[jnp.minimum(me, reqs - 2)]
    tail_length = jnp.where(me > 0, lengths[tail], 0)
    head_length = jnp.where(me + 1 < reqs, lengths[head], 0)
    group_of = (groups[tail], groups[head])
    tail_live = tail_length - tail_length // 2
    tail_first = half_rows - tail_length // 2
    head_first = half_rows - head_length // 2
    near = bias.shape[2]
    head_near = 4 * half_rows // 3
    row = lax.broadcasted_iota(jnp.int32, (half_rows, near), 0)
    column = lax.broadcasted_iota(jnp.int32, (half_rows, near), 1)
    seen = (column >= tail_first) & (column - half_rows <= row)
    bias[0] = jnp.where(seen, 0.0, masked_score)
    own_column = column - (head_near - half_rows)
    seen = (own_column >= head_first) & (own_column <= row)
    bias[1] = jnp.where(seen, 0.0, masked_score)
    slot = lax.broadcasted_iota(jnp.int32, (half_rows, HD), 0)
    value_stage[:, HD:] = jnp.ones((value_stage.shape[0], HD), value_stage.dtype)

    @pl.when(me == 0)
    def _():
        before[...] = jnp.zeros(before.shape, before.dtype)

    for step in range(1, layers + 1):
        relay(0, step)

    @pl.when(me > 0)
    def _():
        before_copy.wait_recv()

    chunks = PER_KV // PAIR
    slots = 2 * chunks
    for h in range(heads):
        from_sibling(h)
        own_columns = slice(h * HD, (h + 1) * HD)
        if h + 2 < heads:
            send_own(h + 2)
        for half in range(2):
            for i in range(per_group):
                block = owners[group_of[half] * per_group + i]
                rows = slice(i * block_rows, (i + 1) * block_rows)
                key_stage[rows, :] = stored[h][block, 0]
                value_stage[rows, :HD] = stored[h][block, 1]
            if half == 0:
                near_rows = near
                for kind, stage in ((0, key_stage), (1, value_stage)):
                    stage[prefix_rows:prefix_rows + half_rows, :HD] = before[kind, :, own_columns]
                    stage[prefix_rows + half_rows:, :HD] = suffix[kind, :half_rows, own_columns]
            else:
                near_rows = head_near
                for kind, stage in ((0, key_stage), (1, value_stage)):
                    stage[prefix_rows:prefix_rows + near_rows, :HD] = suffix[
                        kind, 2 * half_rows - near_rows:, own_columns
                    ]
            live = slot < tail_live if half == 0 else slot >= head_first

            @pl.loop(0, chunks)
            def _(i, half=half, near_rows=near_rows, live=live, h=h):
                span = pl.ds(half * half_rows, half_rows)
                first = (h * PER_KV + i * PAIR) * HD
                places = [pl.ds(pl.multiple_of(first + k * HD, HD), HD) for k in range(PAIR)]
                query = jnp.concatenate([queries[span, place] for place in places], axis=0)
                far = nt_dot(query, key_stage[:prefix_rows, :])
                close = nt_dot(query, key_stage[prefix_rows:prefix_rows + near_rows, :])
                shade = bias[half][:, :near_rows]
                close = close + jnp.concatenate([shade] * PAIR, axis=0)
                top = jnp.maximum(
                    jnp.max(far, axis=1, keepdims=True), jnp.max(close, axis=1, keepdims=True)
                ) * to_exp2
                far = jnp.exp2(far * to_exp2 - top).astype(jnp.bfloat16)
                close = jnp.exp2(close * to_exp2 - top).astype(jnp.bfloat16)
                total = jnp.dot(far, value_stage[:prefix_rows, :], preferred_element_type=jnp.float32)
                total = total + jnp.dot(
                    close, value_stage[prefix_rows:prefix_rows + near_rows, :],
                    preferred_element_type=jnp.float32,
                )
                for k, place in enumerate(places):
                    part = total[k * half_rows:(k + 1) * half_rows]
                    result = jnp.where(live, part[:, :HD] / part[:, HD:], 0.0)
                    out[span, place] = result.astype(out.dtype)
                if h + 1 < heads:
                    done = (half * chunks + i + 1) * layers
                    for k in range(1, max(1, layers // slots) + 1):
                        @pl.when(done % slots == 0)
                        def _(k=k):
                            relay(h + 1, done // slots - max(1, layers // slots) + k)

    @pl.when(me + 1 < reqs)
    def _():
        before_copy.wait_send()

    for h in range(heads):
        for k in range(1, tps):
            peer_copy(h, (tp + k) % tps, tp).wait_send()

        @pl.loop(0, layers)
        def _(layer, h=h):
            mine = layer * 4 + x * 2 + core

            @pl.when((layer <= z) & (z + 1 < layers))
            def _():
                unit_copy(h, mine, UP).wait_send()

            @pl.when((layer >= z) & (z > 0))
            def _():
                unit_copy(h, mine, DOWN).wait_send()

            unit_copy(h, mine, ACROSS).wait_send()
            unit_copy(h, mine, SIBLING).wait_send()
            unit_copy(h, layer * 4 + (1 - x) * 2 + core, SIBLING).wait_send()


def per_device(reqs, tps, queries, suffix, prefix, lengths, groups, order, owners):
    heads = suffix.shape[2] // HD
    rows = queries.shape[0]
    half = rows // 2
    block_rows = prefix.shape[2] * tps
    keys = reqs // GROUPS * block_rows + rows
    vmem = pl.BlockSpec(memory_space=pltpu.VMEM)
    smem = pl.BlockSpec(memory_space=pltpu.SMEM)
    return pl.pallas_call(
        functools.partial(kernel, reqs, tps, heads),
        out_shape=jax.ShapeDtypeStruct(queries.shape, queries.dtype),
        in_specs=[vmem] * 3 + [smem] * 4,
        out_specs=vmem,
        scratch_shapes=[pltpu.VMEM((reqs, 2, block_rows, HD), jnp.bfloat16)] * heads + [
            pltpu.VMEM((2, half, suffix.shape[2]), jnp.bfloat16),
            pltpu.VMEM((keys, HD), jnp.bfloat16),
            pltpu.VMEM((keys, 2 * HD), jnp.bfloat16),
            pltpu.VMEM((2, half, rows), jnp.float32),
            pltpu.SemaphoreType.DMA((heads, reqs, 4)),
            pltpu.SemaphoreType.DMA((heads, reqs)),
            pltpu.SemaphoreType.DMA((heads, tps)),
            pltpu.SemaphoreType.DMA((heads, tps)),
            pltpu.SemaphoreType.DMA((heads,)),
            pltpu.SemaphoreType.DMA,
            pltpu.SemaphoreType.DMA,
        ],
        compiler_params=pltpu.CompilerParams(
            collective_id=0, has_side_effects=True, vmem_limit_bytes=56 * 1024 * 1024
        ),
        cost_estimate=pl.CostEstimate(
            flops=4 * rows * heads * PER_KV * HD * keys,
            bytes_accessed=4 * queries.size,
            transcendentals=rows * heads * PER_KV * keys,
        ),
    )(queries, suffix, prefix, lengths, groups, order, owners)


def solution(mesh):
    in_specs = (
        P("req", "tp"),
        P(None, "req", "tp"),
        P(None, "req", "tp", None),
        P(),
        P(),
        P(),
        P(),
    )
    body = functools.partial(per_device, mesh.shape["req"], mesh.shape["tp"])
    return jax.shard_map(
        body, mesh=mesh, in_specs=in_specs, out_specs=P("req", "tp"), check_vma=False
    )
```

time: 592 us -> 102 us (0.17)
  matrix products: 249 us -> 0 us
  other arithmetic: 125 us -> 0 us
  waiting for transfers between devices: 101 us -> 0 us
  Pallas kernels: 0 us -> 97.6 us
  local copies, waits for them, and re-layouts: 88.1 us -> 3.91 us
  between operations: 13.6 us -> 0.01 us
  starting transfers between devices: 11.7 us -> 0 us
    dot_general x18 -> x0, matrix products: 249 us -> none  [the longest x9 149 us: absorb(): jnp.einsum('jtqk,kjd->jtqd', weights.astype(jnp.bfloat16), value_rows, pr...]
    reduce_sum x14 -> x0, other arithmetic: 110 us -> none  [the longest x9 110 us: absorb(): new_sum = running_sum * shrink + jnp.sum(weights, axis=-1)]
    pallas_call x0 -> x1, Pallas kernels: none -> 97.6 us  [per_device(): pl.pallas_call(functools.partial(kernel, reqs, tps, heads), out_shape=jax...]
    all_to_all x1 -> x0, waiting for transfers between devices: 55 us -> none  [per_device(): lax.all_to_all(stored, 'tp', split_axis=3, concat_axis=2, tiled=True)]
    all_gather x1 -> x0, waiting for transfers between devices: 40.6 us -> none  [per_device(): stored = lax.all_gather(prefix_kv, 'req', axis=1, tiled=True)]
    dynamic_slice x16 -> x0, local copies, waits for them, and re-layouts: 24.7 us -> none  [per_device(): lax.scan(visit_block, status, (key_rows, value_rows, key_groups))]
    another operation x2 -> x0, local copies, waits for them, and re-layouts: 13.8 us -> none  [the longest x1 6.94 us: per_device(): key_rows = relaid[0].reshape(passes, stride * block_rows, kv_heads, HD)]
    all_to_all x1 -> x0, local copies, waits for them, and re-layouts: 13.8 us -> none  [per_device(): lax.all_to_all(stored, 'tp', split_axis=3, concat_axis=2, tiled=True)]
  transfers between devices with their start and end apart: 3 -> 0, of which waited for: 3 -> 0; matrix products, arithmetic and copies ran while one was open for 12% -> 0% of each run, Pallas kernels for 0% -> 0%
where the time goes in v1:
time: 102 us; the launch traced here: 101 us
  Pallas kernels  97.6 us (96%)
  local copies, waits for them, and re-layouts  3.91 us (4%)
    pallas_call x1, Pallas kernels, per_device(): pl.pallas_call(functools.partial(kernel, reqs, tps, heads), out_shape=jax...  97.6 us
    unnamed x1, local copies, waits for them, and re-layouts  3.91 us

profile of v1, /device:TPU:1, one launch (start us, length us, event | category | flops | bytes accessed | tf_op | source)
XLA Modules:
  0.0 101.5 jit_solution(5388729506729103788)
XLA Ops:
  0.0 97.6 %shard_map.73 = bf16[384,4096]{1,0:T(8,128)(2,1)} custom-call(bf16[384,4096]{1,0:T(8,128)(2,1)} %queries.1, bf16[2,384,512]{2,1,0:T(8,128)(2,1)} %suffix.1, bf16[2,1,128,1024]{3,2,1,0:T(8,128)(2,1)} %prefix.1, s32[15]{0:T(128)} %lengths.1, s32[15]{0:T(128)} %groups.1, s32[15]{0:T(128)} %order.1, s32[16]{0:T(128)} %owners.1), custom_call_target="tpu_custom_call" | custom-call | flops 8858370048 | bytes 6291456 | tf_op jit(solution)/shard_map/pallas_call | solution.py:294
  97.6 3.9 %copy.9 = bf16[384,4096]{1,0:T(8,128)(2,1)} copy(bf16[384,4096]{1,0:T(8,128)(2,1)} %shard_map.73) | data formatting | bytes 6291456

commit v2 on v1

--- a/solution.py
+++ b/solution.py
@@ -14,6 +14,7 @@
 GROUPS = 4
 PER_KV = QH // KVH
 PAIR = 2
+STREAMS = 2
 UP, DOWN, ACROSS, SIBLING = range(4)
 
 masked_score = -1e30
@@ -201,7 +202,7 @@
     def _():
         before_copy.wait_recv()
 
-    chunks = PER_KV // PAIR
+    chunks = PER_KV // (PAIR * STREAMS)
     slots = 2 * chunks
     for h in range(heads):
         from_sibling(h)
@@ -230,27 +231,37 @@
             @pl.loop(0, chunks)
             def _(i, half=half, near_rows=near_rows, live=live, h=h):
                 span = pl.ds(half * half_rows, half_rows)
-                first = (h * PER_KV + i * PAIR) * HD
-                places = [pl.ds(pl.multiple_of(first + k * HD, HD), HD) for k in range(PAIR)]
-                query = jnp.concatenate([queries[span, place] for place in places], axis=0)
-                far = nt_dot(query, key_stage[:prefix_rows, :])
-                close = nt_dot(query, key_stage[prefix_rows:prefix_rows + near_rows, :])
-                shade = bias[half][:, :near_rows]
-                close = close + jnp.concatenate([shade] * PAIR, axis=0)
-                top = jnp.maximum(
-                    jnp.max(far, axis=1, keepdims=True), jnp.max(close, axis=1, keepdims=True)
-                ) * to_exp2
-                far = jnp.exp2(far * to_exp2 - top).astype(jnp.bfloat16)
-                close = jnp.exp2(close * to_exp2 - top).astype(jnp.bfloat16)
-                total = jnp.dot(far, value_stage[:prefix_rows, :], preferred_element_type=jnp.float32)
-                total = total + jnp.dot(
-                    close, value_stage[prefix_rows:prefix_rows + near_rows, :],
-                    preferred_element_type=jnp.float32,
-                )
-                for k, place in enumerate(places):
-                    part = total[k * half_rows:(k + 1) * half_rows]
-                    result = jnp.where(live, part[:, :HD] / part[:, HD:], 0.0)
-                    out[span, place] = result.astype(out.dtype)
+                first = (h * PER_KV + i * PAIR * STREAMS) * HD
+                places = [
+                    pl.ds(pl.multiple_of(first + k * HD, HD), HD) for k in range(PAIR * STREAMS)
+                ]
+                shade = jnp.concatenate([bias[half][:, :near_rows]] * PAIR, axis=0)
+                scores = []
+                for stream in range(STREAMS):
+                    pair = places[stream * PAIR:(stream + 1) * PAIR]
+                    query = jnp.concatenate([queries[span, place] for place in pair], axis=0)
+                    far = nt_dot(query, key_stage[:prefix_rows, :])
+                    close = nt_dot(query, key_stage[prefix_rows:prefix_rows + near_rows, :])
+                    scores.append((far, close + shade))
+                for stream in range(STREAMS):
+                    pair = places[stream * PAIR:(stream + 1) * PAIR]
+                    far, close = scores[stream]
+                    top = jnp.maximum(
+                        jnp.max(far, axis=1, keepdims=True), jnp.max(close, axis=1, keepdims=True)
+                    ) * to_exp2
+                    far = jnp.exp2(far * to_exp2 - top).astype(jnp.bfloat16)
+                    close = jnp.exp2(close * to_exp2 - top).astype(jnp.bfloat16)
+                    total = jnp.dot(
+                        far, value_stage[:prefix_rows, :], preferred_element_type=jnp.float32
+                    )
+                    total = total + jnp.dot(
+                        close, value_stage[prefix_rows:prefix_rows + near_rows, :],
+                        preferred_element_type=jnp.float32,
+                    )
+                    for k, place in enumerate(pair):
+                        part = total[k * half_rows:(k + 1) * half_rows]
+                        result = jnp.where(live, part[:, :HD] / part[:, HD:], 0.0)
+                        out[span, place] = result.astype(out.dtype)
                 if h + 1 < heads:
                     done = (half * chunks + i + 1) * layers
                     for k in range(1, max(1, layers // slots) + 1):

time: 102 us -> 92.7 us (0.909)
  Pallas kernels: 97.6 us -> 88.7 us
    pallas_call x1, Pallas kernels: 97.6 us -> 88.7 us  [per_device(): pl.pallas_call(functools.partial(kernel, reqs, tps, heads), out_shape=jax...]
where the time goes in v2:
time: 92.7 us; the launch traced here: 92.6 us
  Pallas kernels  88.7 us (96%)
  local copies, waits for them, and re-layouts  3.91 us (4%)
    pallas_call x1, Pallas kernels, per_device(): pl.pallas_call(functools.partial(kernel, reqs, tps, heads), out_shape=jax...  88.7 us
    unnamed x1, local copies, waits for them, and re-layouts  3.91 us

profile of v2, /device:TPU:1, one launch (start us, length us, event | category | flops | bytes accessed | tf_op | source)
XLA Modules:
  0.0 92.6 jit_solution(761235219865121666)
XLA Ops:
  0.0 88.7 %shard_map.73 = bf16[384,4096]{1,0:T(8,128)(2,1)} custom-call(bf16[384,4096]{1,0:T(8,128)(2,1)} %queries.1, bf16[2,384,512]{2,1,0:T(8,128)(2,1)} %suffix.1, bf16[2,1,128,1024]{3,2,1,0:T(8,128)(2,1)} %prefix.1, s32[15]{0:T(128)} %lengths.1, s32[15]{0:T(128)} %groups.1, s32[15]{0:T(128)} %order.1, s32[16]{0:T(128)} %owners.1), custom_call_target="tpu_custom_call" | custom-call | flops 8858370048 | bytes 6291456 | tf_op jit(solution)/shard_map/pallas_call | solution.py:305
  88.7 3.9 %copy.9 = bf16[384,4096]{1,0:T(8,128)(2,1)} copy(bf16[384,4096]{1,0:T(8,128)(2,1)} %shard_map.73) | data formatting | bytes 6291456

commit v3 on v2

--- a/solution.py
+++ b/solution.py
@@ -213,19 +213,24 @@
             for i in range(per_group):
                 block = owners[group_of[half] * per_group + i]
                 rows = slice(i * block_rows, (i + 1) * block_rows)
-                key_stage[rows, :] = stored[h][block, 0]
+                turned = stored[h][block, 0].T
+                key_stage[:HD, rows] = turned
+                key_stage[HD:, rows] = turned
                 value_stage[rows, :HD] = stored[h][block, 1]
+            near_rows = near if half == 0 else head_near
             if half == 0:
-                near_rows = near
-                for kind, stage in ((0, key_stage), (1, value_stage)):
-                    stage[prefix_rows:prefix_rows + half_rows, :HD] = before[kind, :, own_columns]
-                    stage[prefix_rows + half_rows:, :HD] = suffix[kind, :half_rows, own_columns]
+                close = [
+                    jnp.concatenate(
+                        [before[kind, :, own_columns], suffix[kind, :half_rows, own_columns]], axis=0
+                    ) for kind in range(2)
+                ]
             else:
-                near_rows = head_near
-                for kind, stage in ((0, key_stage), (1, value_stage)):
-                    stage[prefix_rows:prefix_rows + near_rows, :HD] = suffix[
-                        kind, 2 * half_rows - near_rows:, own_columns
-                    ]
+                close = [suffix[kind, 2 * half_rows - near_rows:, own_columns] for kind in range(2)]
+            rows = slice(prefix_rows, prefix_rows + near_rows)
+            turned = close[0].T
+            key_stage[:HD, rows] = turned
+            key_stage[HD:, rows] = turned
+            value_stage[rows, :HD] = close[1]
             live = slot < tail_live if half == 0 else slot >= head_first
 
             @pl.loop(0, chunks)
@@ -236,27 +241,30 @@
                     pl.ds(pl.multiple_of(first + k * HD, HD), HD) for k in range(PAIR * STREAMS)
                 ]
                 shade = jnp.concatenate([bias[half][:, :near_rows]] * PAIR, axis=0)
+                rows = prefix_rows + near_rows
                 scores = []
                 for stream in range(STREAMS):
                     pair = places[stream * PAIR:(stream + 1) * PAIR]
                     query = jnp.concatenate([queries[span, place] for place in pair], axis=0)
-                    far = nt_dot(query, key_stage[:prefix_rows, :])
-                    close = nt_dot(query, key_stage[prefix_rows:prefix_rows + near_rows, :])
-                    scores.append((far, close + shade))
+                    query = query.astype(jnp.float32) * to_exp2
+                    high = query.astype(jnp.bfloat16)
+                    low = (query - high.astype(jnp.float32)).astype(jnp.bfloat16)
+                    scores.append(jnp.dot(
+                        jnp.concatenate([high, low], axis=1), key_stage[:, :rows],
+                        preferred_element_type=jnp.float32,
+                    ))
                 for stream in range(STREAMS):
                     pair = places[stream * PAIR:(stream + 1) * PAIR]
-                    far, close = scores[stream]
-                    top = jnp.maximum(
-                        jnp.max(far, axis=1, keepdims=True), jnp.max(close, axis=1, keepdims=True)
-                    ) * to_exp2
-                    far = jnp.exp2(far * to_exp2 - top).astype(jnp.bfloat16)
-                    close = jnp.exp2(close * to_exp2 - top).astype(jnp.bfloat16)
+                    far, close = scores[stream][:, :prefix_rows], scores[stream][:, prefix_rows:] + shade
+                    lanes = [far[:, k:k + HD] for k in range(0, prefix_rows, HD)]
+                    lanes += [close[:, k:k + HD] for k in range(0, near_rows, HD)]
+                    top = jnp.max(functools.reduce(jnp.maximum, lanes), axis=1, keepdims=True)
+                    weights = jnp.concatenate([
+                        jnp.exp2(far - top).astype(jnp.bfloat16),
+                        jnp.exp2(close - top).astype(jnp.bfloat16),
+                    ], axis=1)
                     total = jnp.dot(
-                        far, value_stage[:prefix_rows, :], preferred_element_type=jnp.float32
-                    )
-                    total = total + jnp.dot(
-                        close, value_stage[prefix_rows:prefix_rows + near_rows, :],
-                        preferred_element_type=jnp.float32,
+                        weights, value_stage[:rows, :], preferred_element_type=jnp.float32
                     )
                     for k, place in enumerate(pair):
                         part = total[k * half_rows:(k + 1) * half_rows]
@@ -309,7 +317,7 @@
         out_specs=vmem,
         scratch_shapes=[pltpu.VMEM((reqs, 2, block_rows, HD), jnp.bfloat16)] * heads + [
             pltpu.VMEM((2, half, suffix.shape[2]), jnp.bfloat16),
-            pltpu.VMEM((keys, HD), jnp.bfloat16),
+            pltpu.VMEM((2 * HD, keys), jnp.bfloat16),
             pltpu.VMEM((keys, 2 * HD), jnp.bfloat16),
             pltpu.VMEM((2, half, rows), jnp.float32),
             pltpu.SemaphoreType.DMA((heads, reqs, 4)),

time: 92.7 us -> 93.6 us (level)
  no operation moved by 1% of the time
where the time goes in v3:
time: 93.6 us; the launch traced here: 93.5 us
  Pallas kernels  89.6 us (96%)
  local copies, waits for them, and re-layouts  3.91 us (4%)
    pallas_call x1, Pallas kernels, per_device(): pl.pallas_call(functools.partial(kernel, reqs, tps, heads), out_shape=jax...  89.6 us
    unnamed x1, local copies, waits for them, and re-layouts  3.91 us

profile of v3, /device:TPU:1, one launch (start us, length us, event | category | flops | bytes accessed | tf_op | source)
XLA Modules:
  0.0 93.5 jit_solution(6789648322237667804)
XLA Ops:
  0.0 89.6 %shard_map.73 = bf16[384,4096]{1,0:T(8,128)(2,1)} custom-call(bf16[384,4096]{1,0:T(8,128)(2,1)} %queries.1, bf16[2,384,512]{2,1,0:T(8,128)(2,1)} %suffix.1, bf16[2,1,128,1024]{3,2,1,0:T(8,128)(2,1)} %prefix.1, s32[15]{0:T(128)} %lengths.1, s32[15]{0:T(128)} %groups.1, s32[15]{0:T(128)} %order.1, s32[16]{0:T(128)} %owners.1), custom_call_target="tpu_custom_call" | custom-call | flops 8858370048 | bytes 6291456 | tf_op jit(solution)/shard_map/pallas_call | solution.py:313
  89.6 3.9 %copy.9 = bf16[384,4096]{1,0:T(8,128)(2,1)} copy(bf16[384,4096]{1,0:T(8,128)(2,1)} %shard_map.73) | data formatting | bytes 6291456

commit v4 on v3

--- a/solution.py
+++ b/solution.py
@@ -13,8 +13,9 @@
 HD = 128
 GROUPS = 4
 PER_KV = QH // KVH
-PAIR = 2
-STREAMS = 2
+PAIR = 4
+TILE = 256
+BLOCK = 16
 UP, DOWN, ACROSS, SIBLING = range(4)
 
 masked_score = -1e30
@@ -32,7 +33,7 @@
     *scratch,
 ):
     stored = scratch[:heads]
-    (before, key_stage, value_stage, bias,
+    (before, key_stage, value_stage, bias, scores, weights,
      unit_send, unit_recv, peer_send, peer_recv, own_sem, before_send, before_recv) = scratch[heads:]
     me = lax.axis_index("req")
     tp = lax.axis_index("tp")
@@ -202,7 +203,7 @@
     def _():
         before_copy.wait_recv()
 
-    chunks = PER_KV // (PAIR * STREAMS)
+    chunks = PER_KV // PAIR
     slots = 2 * chunks
     for h in range(heads):
         from_sibling(h)
@@ -236,40 +237,36 @@
             @pl.loop(0, chunks)
             def _(i, half=half, near_rows=near_rows, live=live, h=h):
                 span = pl.ds(half * half_rows, half_rows)
-                first = (h * PER_KV + i * PAIR * STREAMS) * HD
+                first = (h * PER_KV + i * PAIR) * HD
                 places = [
-                    pl.ds(pl.multiple_of(first + k * HD, HD), HD) for k in range(PAIR * STREAMS)
+                    pl.ds(pl.multiple_of(first + k * HD, HD), HD) for k in range(PAIR)
                 ]
                 shade = jnp.concatenate([bias[half][:, :near_rows]] * PAIR, axis=0)
                 rows = prefix_rows + near_rows
-                scores = []
-                for stream in range(STREAMS):
-                    pair = places[stream * PAIR:(stream + 1) * PAIR]
-                    query = jnp.concatenate([queries[span, place] for place in pair], axis=0)
-                    query = query.astype(jnp.float32) * to_exp2
-                    high = query.astype(jnp.bfloat16)
-                    low = (query - high.astype(jnp.float32)).astype(jnp.bfloat16)
-                    scores.append(jnp.dot(
-                        jnp.concatenate([high, low], axis=1), key_stage[:, :rows],
-                        preferred_element_type=jnp.float32,
-                    ))
-                for stream in range(STREAMS):
-                    pair = places[stream * PAIR:(stream + 1) * PAIR]
-                    far, close = scores[stream][:, :prefix_rows], scores[stream][:, prefix_rows:] + shade
-                    lanes = [far[:, k:k + HD] for k in range(0, prefix_rows, HD)]
-                    lanes += [close[:, k:k + HD] for k in range(0, near_rows, HD)]
+                query = jnp.concatenate([queries[span, place] for place in places], axis=0)
+                query = query.astype(jnp.float32) * to_exp2
+                high = query.astype(jnp.bfloat16)
+                low = (query - high.astype(jnp.float32)).astype(jnp.bfloat16)
+                query = jnp.concatenate([high, low], axis=1)
+                for first in range(0, rows, TILE):
+                    tile = slice(first, min(first + TILE, rows))
+                    part = jnp.dot(query, key_stage[:, tile], preferred_element_type=jnp.float32)
+                    if first >= prefix_rows:
+                        part = part + shade[:, first - prefix_rows:tile.stop - prefix_rows]
+                    scores[:, tile] = part
+                for first in range(0, scores.shape[0], BLOCK):
+                    block = slice(first, first + BLOCK)
+                    score = scores[block, :rows]
+                    lanes = [score[:, k:k + HD] for k in range(0, rows, HD)]
                     top = jnp.max(functools.reduce(jnp.maximum, lanes), axis=1, keepdims=True)
-                    weights = jnp.concatenate([
-                        jnp.exp2(far - top).astype(jnp.bfloat16),
-                        jnp.exp2(close - top).astype(jnp.bfloat16),
-                    ], axis=1)
-                    total = jnp.dot(
-                        weights, value_stage[:rows, :], preferred_element_type=jnp.float32
-                    )
-                    for k, place in enumerate(pair):
-                        part = total[k * half_rows:(k + 1) * half_rows]
-                        result = jnp.where(live, part[:, :HD] / part[:, HD:], 0.0)
-                        out[span, place] = result.astype(out.dtype)
+                    weights[block, :rows] = jnp.exp2(score - top).astype(jnp.bfloat16)
+                total = jnp.dot(
+                    weights[:, :rows], value_stage[:rows, :], preferred_element_type=jnp.float32
+                )
+                for k, place in enumerate(places):
+                    part = total[k * half_rows:(k + 1) * half_rows]
+                    result = jnp.where(live, part[:, :HD] / part[:, HD:], 0.0)
+                    out[span, place] = result.astype(out.dtype)
                 if h + 1 < heads:
                     done = (half * chunks + i + 1) * layers
                     for k in range(1, max(1, layers // slots) + 1):
@@ -320,6 +317,8 @@
             pltpu.VMEM((2 * HD, keys), jnp.bfloat16),
             pltpu.VMEM((keys, 2 * HD), jnp.bfloat16),
             pltpu.VMEM((2, half, rows), jnp.float32),
+            pltpu.VMEM((PAIR * half, keys), jnp.float32),
+            pltpu.VMEM((PAIR * half, keys), jnp.bfloat16),
             pltpu.SemaphoreType.DMA((heads, reqs, 4)),
             pltpu.SemaphoreType.DMA((heads, reqs)),
             pltpu.SemaphoreType.DMA((heads, tps)),

time: 93.6 us -> 102 us (1.090)
  Pallas kernels: 89.6 us -> 98.4 us
    pallas_call x1, Pallas kernels: 89.6 us -> 98.4 us  [per_device(): pl.pallas_call(functools.partial(kernel, reqs, tps, heads), out_shape=jax...]
where the time goes in v4:
time: 102 us
  Pallas kernels  98.4 us (96%)
  local copies, waits for them, and re-layouts  3.91 us (4%)
    pallas_call x1, Pallas kernels, per_device(): pl.pallas_call(functools.partial(kernel, reqs, tps, heads), out_shape=jax...  98.4 us
    unnamed x1, local copies, waits for them, and re-layouts  3.91 us

profile of v4, /device:TPU:1, one launch (start us, length us, event | category | flops | bytes accessed | tf_op | source)
XLA Modules:
  0.0 102.3 jit_solution(6514254923405716977)
XLA Ops:
  0.0 98.4 %shard_map.73 = bf16[384,4096]{1,0:T(8,128)(2,1)} custom-call(bf16[384,4096]{1,0:T(8,128)(2,1)} %queries.1, bf16[2,384,512]{2,1,0:T(8,128)(2,1)} %suffix.1, bf16[2,1,128,1024]{3,2,1,0:T(8,128)(2,1)} %prefix.1, s32[15]{0:T(128)} %lengths.1, s32[15]{0:T(128)} %groups.1, s32[15]{0:T(128)} %order.1, s32[16]{0:T(128)} %owners.1), custom_call_target="tpu_custom_call" | custom-call | flops 8858370048 | bytes 6291456 | tf_op jit(solution)/shard_map/pallas_call | solution.py:310
  98.4 3.9 %copy.9 = bf16[384,4096]{1,0:T(8,128)(2,1)} copy(bf16[384,4096]{1,0:T(8,128)(2,1)} %shard_map.73) | data formatting | bytes 6291456

commit v5 on v1

--- a/solution.py
+++ b/solution.py
@@ -14,6 +14,7 @@
 GROUPS = 4
 PER_KV = QH // KVH
 PAIR = 2
+STREAMS = 2
 UP, DOWN, ACROSS, SIBLING = range(4)
 
 masked_score = -1e30
@@ -179,12 +180,11 @@
     tail_first = half_rows - tail_length // 2
     head_first = half_rows - head_length // 2
     near = bias.shape[2]
-    head_near = 4 * half_rows // 3
     row = lax.broadcasted_iota(jnp.int32, (half_rows, near), 0)
     column = lax.broadcasted_iota(jnp.int32, (half_rows, near), 1)
     seen = (column >= tail_first) & (column - half_rows <= row)
     bias[0] = jnp.where(seen, 0.0, masked_score)
-    own_column = column - (head_near - half_rows)
+    own_column = column - (near - half_rows)
     seen = (own_column >= head_first) & (own_column <= row)
     bias[1] = jnp.where(seen, 0.0, masked_score)
     slot = lax.broadcasted_iota(jnp.int32, (half_rows, HD), 0)
@@ -201,62 +201,98 @@
     def _():
         before_copy.wait_recv()
 
-    chunks = PER_KV // PAIR
+    chunks = PER_KV // (PAIR * STREAMS)
     slots = 2 * chunks
-    for h in range(heads):
-        from_sibling(h)
-        own_columns = slice(h * HD, (h + 1) * HD)
-        if h + 2 < heads:
-            send_own(h + 2)
-        for half in range(2):
-            for i in range(per_group):
-                block = owners[group_of[half] * per_group + i]
-                rows = slice(i * block_rows, (i + 1) * block_rows)
-                key_stage[rows, :] = stored[h][block, 0]
-                value_stage[rows, :HD] = stored[h][block, 1]
-            if half == 0:
-                near_rows = near
-                for kind, stage in ((0, key_stage), (1, value_stage)):
-                    stage[prefix_rows:prefix_rows + half_rows, :HD] = before[kind, :, own_columns]
-                    stage[prefix_rows + half_rows:, :HD] = suffix[kind, :half_rows, own_columns]
-            else:
-                near_rows = head_near
-                for kind, stage in ((0, key_stage), (1, value_stage)):
-                    stage[prefix_rows:prefix_rows + near_rows, :HD] = suffix[
-                        kind, 2 * half_rows - near_rows:, own_columns
-                    ]
-            live = slot < tail_live if half == 0 else slot >= head_first
-
-            @pl.loop(0, chunks)
-            def _(i, half=half, near_rows=near_rows, live=live, h=h):
-                span = pl.ds(half * half_rows, half_rows)
-                first = (h * PER_KV + i * PAIR) * HD
-                places = [pl.ds(pl.multiple_of(first + k * HD, HD), HD) for k in range(PAIR)]
-                query = jnp.concatenate([queries[span, place] for place in places], axis=0)
-                far = nt_dot(query, key_stage[:prefix_rows, :])
-                close = nt_dot(query, key_stage[prefix_rows:prefix_rows + near_rows, :])
-                shade = bias[half][:, :near_rows]
-                close = close + jnp.concatenate([shade] * PAIR, axis=0)
-                top = jnp.maximum(
-                    jnp.max(far, axis=1, keepdims=True), jnp.max(close, axis=1, keepdims=True)
-                ) * to_exp2
-                far = jnp.exp2(far * to_exp2 - top).astype(jnp.bfloat16)
-                close = jnp.exp2(close * to_exp2 - top).astype(jnp.bfloat16)
-                total = jnp.dot(far, value_stage[:prefix_rows, :], preferred_element_type=jnp.float32)
-                total = total + jnp.dot(
-                    close, value_stage[prefix_rows:prefix_rows + near_rows, :],
+    @pl.loop(0, 2 * heads)
+    def _(turn):
+        h, half = turn // 2, turn % 2
+        group = jnp.where(half == 0, group_of[0], group_of[1])
+        for k in range(heads):
+            @pl.when(turn == 2 * k)
+            def _(k=k):
+                from_sibling(k)
+                if k + 2 < heads:
+                    send_own(k + 2)
+
+            @pl.when(h == k)
+            def _(k=k):
+                for i in range(per_group):
+                    block = owners[group * per_group + i]
+                    rows = slice(i * block_rows, (i + 1) * block_rows)
+                    turned = stored[k][block, 0].T
+                    key_stage[:HD, rows] = turned
+                    key_stage[HD:, rows] = turned
+                    value_stage[rows, :HD] = stored[k][block, 1]
+
+        own_columns = pl.ds(pl.multiple_of(h * HD, HD), HD)
+        rows = slice(prefix_rows, prefix_rows + near)
+
+        def stage_near(keys, values):
+            turned = keys.T
+            key_stage[:HD, rows] = turned
+            key_stage[HD:, rows] = turned
+            value_stage[rows, :HD] = values
+
+        @pl.when(half == 0)
+        def _():
+            stage_near(*[
+                jnp.concatenate(
+                    [before[kind, :, own_columns], suffix[kind, :half_rows, own_columns]], axis=0
+                ) for kind in range(2)
+            ])
+
+        @pl.when(half == 1)
+        def _():
+            stage_near(suffix[0, :, own_columns], suffix[1, :, own_columns])
+
+        live = (slot >= jnp.where(half == 0, 0, head_first)) & (
+            slot < jnp.where(half == 0, tail_live, half_rows)
+        )
+
+        @pl.loop(0, chunks)
+        def _(i):
+            span = pl.ds(pl.multiple_of(half * half_rows, half_rows), half_rows)
+            first = (h * PER_KV + i * PAIR * STREAMS) * HD
+            places = [
+                pl.ds(pl.multiple_of(first + k * HD, HD), HD) for k in range(PAIR * STREAMS)
+            ]
+            shade = jnp.concatenate([bias[half]] * PAIR, axis=0)
+            rows = prefix_rows + near
+            scores = []
+            for stream in range(STREAMS):
+                pair = places[stream * PAIR:(stream + 1) * PAIR]
+                query = jnp.concatenate([queries[span, place] for place in pair], axis=0)
+                query = query.astype(jnp.float32) * to_exp2
+                high = query.astype(jnp.bfloat16)
+                low = (query - high.astype(jnp.float32)).astype(jnp.bfloat16)
+                scores.append(jnp.dot(
+                    jnp.concatenate([high, low], axis=1), key_stage[:, :rows],
                     preferred_element_type=jnp.float32,
+                ))
+            for stream in range(STREAMS):
+                pair = places[stream * PAIR:(stream + 1) * PAIR]
+                far, close = scores[stream][:, :prefix_rows], scores[stream][:, prefix_rows:] + shade
+                lanes = [far[:, k:k + HD] for k in range(0, prefix_rows, HD)]
+                lanes += [close[:, k:k + HD] for k in range(0, near, HD)]
+                top = jnp.max(functools.reduce(jnp.maximum, lanes), axis=1, keepdims=True)
+                weights = jnp.concatenate([
+                    jnp.exp2(far - top).astype(jnp.bfloat16),
+                    jnp.exp2(close - top).astype(jnp.bfloat16),
+                ], axis=1)
+                total = jnp.dot(
+                    weights, value_stage[:rows, :], preferred_element_type=jnp.float32
                 )
-                for k, place in enumerate(places):
+                for k, place in enumerate(pair):
                     part = total[k * half_rows:(k + 1) * half_rows]
                     result = jnp.where(live, part[:, :HD] / part[:, HD:], 0.0)
                     out[span, place] = result.astype(out.dtype)
-                if h + 1 < heads:
-                    done = (half * chunks + i + 1) * layers
-                    for k in range(1, max(1, layers // slots) + 1):
-                        @pl.when(done % slots == 0)
-                        def _(k=k):
-                            relay(h + 1, done // slots - max(1, layers // slots) + k)
+            done = (half * chunks + i + 1) * layers
+            steps = max(1, layers // slots)
+            for later in range(1, heads):
+                @pl.when((h + 1 == later) & (done % slots == 0))
+                def _(later=later):
+                    for k in range(1, steps + 1):
+                        relay(later, done // slots - steps + k)
 
     @pl.when(me + 1 < reqs)
     def _():
@@ -298,7 +334,7 @@
         out_specs=vmem,
         scratch_shapes=[pltpu.VMEM((reqs, 2, block_rows, HD), jnp.bfloat16)] * heads + [
             pltpu.VMEM((2, half, suffix.shape[2]), jnp.bfloat16),
-            pltpu.VMEM((keys, HD), jnp.bfloat16),
+            pltpu.VMEM((2 * HD, keys), jnp.bfloat16),
             pltpu.VMEM((keys, 2 * HD), jnp.bfloat16),
             pltpu.VMEM((2, half, rows), jnp.float32),
             pltpu.SemaphoreType.DMA((heads, reqs, 4)),

time: 102 us -> 94.3 us (0.925)
  Pallas kernels: 97.6 us -> 90.2 us
    pallas_call x1, Pallas kernels: 97.6 us -> 90.2 us  [per_device(): pl.pallas_call(functools.partial(kernel, reqs, tps, heads), out_shape=jax...]
where the time goes in v5:
time: 94.3 us; the launch traced here: 94.2 us
  Pallas kernels  90.2 us (96%)
  local copies, waits for them, and re-layouts  3.91 us (4%)
    pallas_call x1, Pallas kernels, per_device(): pl.pallas_call(functools.partial(kernel, reqs, tps, heads), out_shape=jax...  90.2 us
    unnamed x1, local copies, waits for them, and re-layouts  3.91 us

profile of v5, /device:TPU:1, one launch (start us, length us, event | category | flops | bytes accessed | tf_op | source)
XLA Modules:
  0.0 94.2 jit_solution(14572212782185142078)
XLA Ops:
  0.0 90.2 %shard_map.73 = bf16[384,4096]{1,0:T(8,128)(2,1)} custom-call(bf16[384,4096]{1,0:T(8,128)(2,1)} %queries.1, bf16[2,384,512]{2,1,0:T(8,128)(2,1)} %suffix.1, bf16[2,1,128,1024]{3,2,1,0:T(8,128)(2,1)} %prefix.1, s32[15]{0:T(128)} %lengths.1, s32[15]{0:T(128)} %groups.1, s32[15]{0:T(128)} %order.1, s32[16]{0:T(128)} %owners.1), custom_call_target="tpu_custom_call" | custom-call | flops 8858370048 | bytes 6291456 | tf_op jit(solution)/shard_map/pallas_call | solution.py:330
  90.3 3.9 %copy.9 = bf16[384,4096]{1,0:T(8,128)(2,1)} copy(bf16[384,4096]{1,0:T(8,128)(2,1)} %shard_map.73) | data formatting | bytes 6291456
